TPU v7x, 512 devices: a whole 4x4x16 slice. The times are simulated.
512 devices in a mesh: wide: 128 (over z, y, core), narrow: 4 (over x).
Axes of the slice: x: 4, y: 4, z: 16, core: 2. Of those that a mesh axis runs over, the one named last changes fastest.
Arguments:
- coefficients: bfloat16 [100, 2097152], P(None, ('wide', 'narrow')), may hold values from -6 to 6
- neighbours: int32 [4, 2097152], P(None, ('wide', 'narrow')), may hold values from 0 to 5119
- halo_blocks: int32 [512, 4, 2], P(('wide', 'narrow')), may hold values from 0 to 31, as said below
- recon_weight: bfloat16 [5, 75, 100], replicated, may hold values from -0.25 to 0.25
- owner_device: int32 [16384], P(('wide', 'narrow')), may hold values from 0 to 511, as said below
- work_count: int32 [16384], P(('wide', 'narrow')), may hold values from 1 to 4
Outputs:
- migrated_modal: bfloat16 [100, 2097152], P(None, ('wide', 'narrow'))
- migrated_metric: float32 [6, 2097152], P(None, ('wide', 'narrow'))
- migrated_work: float32 [2097152], P(('wide', 'narrow'))
Inputs may be any that keep to these rules, and one draw needn't show every extreme that they name: `halo_blocks`: each device's list for one direction holds 2 different block numbers of that device. `owner_device`: every device receives exactly 32 blocks. Of one device's blocks, either exactly 1 or none go to devices of any one wide index. Two devices of the same wide index with narrow indices 2j and 2j + 1 together send either exactly 1 or none of their blocks to devices of any one wide index. For every wide index w and narrow indices a and c, exactly 8 of the blocks that devices of narrow index a send to wide index w go to the device of wide index w and narrow index c.
All inputs are finite; a program needn't handle non-finite values.
Results may differ from a plain program's by a relative error of at most 0.0004.
Values may be sent and summed in bfloat16 or wider, within the bound.
A program may use at most 64 MiB of HBM per device.

v0:
```python
import jax
import jax.numpy as jnp
from jax import lax
from jax.sharding import PartitionSpec as P


def passed_along(value, axis, steps):
    count = lax.axis_size(axis)
    pairs = [(source, (source + steps) % count) for source in range(count)]
    return lax.ppermute(value, axis, pairs)


def swapped(value, axis, apart):
    return lax.ppermute(value, axis, [(i, i ^ 1 << apart) for i in range(lax.axis_size(axis))])


def metric_rows(derivs):
    vectors = derivs.reshape(derivs.shape[0] // 3, 3, derivs.shape[1])
    inverse = 1.0 / vectors.shape[0]
    along_x = vectors[:, 0]
    along_y = vectors[:, 1]
    along_z = vectors[:, 2]
    return jnp.stack(
        [
            1.0 + inverse * jnp.sum(along_x * along_x, axis=0),
            1.0 + inverse * jnp.sum(along_y * along_y, axis=0),
            1.0 + inverse * jnp.sum(along_z * along_z, axis=0),
            inverse * jnp.sum(along_x * along_y, axis=0),
            inverse * jnp.sum(along_x * along_z, axis=0),
            inverse * jnp.sum(along_y * along_z, axis=0),
        ]
    )


def determinant(components):
    metric_xx = components[0]
    metric_yy = components[1]
    metric_zz = components[2]
    metric_xy = components[3]
    metric_xz = components[4]
    metric_yz = components[5]
    return (
        metric_xx * (metric_yy * metric_zz - metric_yz * metric_yz)
        - metric_xy * (metric_xy * metric_zz - metric_yz * metric_xz)
        + metric_xz * (metric_xy * metric_yz - metric_yy * metric_xz)
    )


def first_slots(slot_of, slot_total, position):
    slot_ids = jnp.arange(slot_total, dtype=jnp.int32)
    matches = slot_of[None, :] == slot_ids[:, None]
    filled = jnp.any(matches, axis=1)
    picked = jnp.sum(jnp.where(matches, position[None, :], 0), axis=1)
    return (filled, picked)


def per_device(coefficients, neighbours, halo_blocks, recon_weight, owner_device, work_count):
    coeff_count, elem_count = coefficients.shape
    block_count = owner_device.shape[0]
    block_len = elem_count // block_count
    halo_count = halo_blocks.shape[2]
    wide_size = lax.axis_size("wide")
    narrow_size = lax.axis_size("narrow")
    blocked = coefficients.reshape(coeff_count, block_count, block_len)
    sending = halo_blocks[0]

    def outgoing(direction):
        return jnp.take(blocked, sending[direction], axis=1)

    def from_wide(block_set, offset):
        return passed_along(block_set, "wide", offset)

    def from_narrow(block_set, offset):
        return passed_along(block_set, "narrow", offset)

    arrived = [
        from_wide(outgoing(1), 1),
        from_wide(outgoing(0), -1),
        from_narrow(outgoing(3), 1),
        from_narrow(outgoing(2), -1),
    ]
    halo_cols = jnp.concatenate(arrived, axis=1).reshape(coeff_count, 4 * halo_count * block_len)
    derivs = jnp.dot(recon_weight[0], coefficients, preferred_element_type=jnp.float32)
    extended = jnp.concatenate([coefficients, halo_cols], axis=1)
    for face_index in range(4):
        gathered = jnp.take(extended, neighbours[face_index], axis=1)
        derivs = derivs + jnp.dot(
            recon_weight[face_index + 1], gathered, preferred_element_type=jnp.float32
        )
    components = metric_rows(derivs)
    work_est = jnp.repeat(work_count.astype(jnp.float32), block_len) * jnp.sqrt(
        determinant(components)
    )
    components, work_est = lax.optimization_barrier((components, work_est))
    stats = jnp.concatenate([components, work_est[None, :]], axis=0).reshape(
        7, block_count, block_len
    )
    wide_target = owner_device // narrow_size
    narrow_target = owner_device % narrow_size
    position = jnp.arange(block_count, dtype=jnp.int32)
    earlier = (wide_target[None, :] == wide_target[:, None]) & (
        position[None, :] < position[:, None]
    )
    rank_of = jnp.sum(earlier.astype(jnp.int32), axis=1)
    member = lax.axis_index("narrow") % 2
    other = 1 - member
    half_len = block_len // 2
    pair_wide = max(1, 2 * block_count // wide_size)
    pair_total = wide_size * pair_wide
    pair_ids = jnp.arange(pair_total, dtype=jnp.int32)
    pair_slot = wide_target * pair_wide + rank_of
    own_coeffs = lax.dynamic_slice_in_dim(blocked, member * half_len, half_len, 2)
    own_stats = lax.dynamic_slice_in_dim(stats, member * half_len, half_len, 2)
    give_coeffs = lax.dynamic_slice_in_dim(blocked, other * half_len, half_len, 2)
    give_stats = lax.dynamic_slice_in_dim(stats, other * half_len, half_len, 2)
    labels = jnp.stack([pair_slot, narrow_target]).astype(jnp.float32)
    partner_coeffs = swapped(give_coeffs, "narrow", 0)
    partner_stats, partner_labels = swapped((give_stats, labels), "narrow", 0)
    partner_slot = partner_labels[0].astype(jnp.int32)
    partner_target = partner_labels[1].astype(jnp.int32)
    own_has, own_pick = first_slots(pair_slot, pair_total, position)
    partner_has, partner_pick = first_slots(partner_slot, pair_total, position)
    zero_coeff = jnp.zeros((), blocked.dtype)
    joined_coeffs = jnp.where(
        own_has[None, :, None],
        jnp.take(own_coeffs, own_pick, axis=1),
        jnp.where(
            partner_has[None, :, None], jnp.take(partner_coeffs, partner_pick, axis=1), zero_coeff
        ),
    )
    joined_stats = jnp.where(
        own_has[None, :, None],
        jnp.take(own_stats, own_pick, axis=1),
        jnp.where(partner_has[None, :, None], jnp.take(partner_stats, partner_pick, axis=1), 0.0),
    )
    pair_tags = jnp.where(
        own_has,
        jnp.take(narrow_target, own_pick) * 2 + member,
        jnp.where(partner_has, jnp.take(partner_target, partner_pick) * 2 + other, -1),
    )
    stats_in, tags_in = (
        lax.all_to_all(joined_stats, "wide", split_axis=1, concat_axis=1, tiled=True),
        lax.all_to_all(
            pair_tags.astype(jnp.float32)[None, :], "wide", split_axis=1, concat_axis=1, tiled=True
        ),
    )
    coeffs_in = lax.all_to_all(joined_coeffs, "wide", split_axis=1, concat_axis=1, tiled=True)
    arrived_tags = tags_in[0].astype(jnp.int32)
    anchor = jnp.where(arrived_tags >= 0, arrived_tags % 2, -1)
    keep_order = jnp.argsort(jnp.where(anchor == member, 0, 1) * pair_total + pair_ids)[
        :block_count
    ]
    pass_order = jnp.argsort(jnp.where(anchor == other, 0, 1) * pair_total + pair_ids)[:block_count]
    returned_coeffs = swapped(jnp.take(coeffs_in, pass_order, axis=1), "narrow", 0)
    returned_stats = swapped(jnp.take(stats_in, pass_order, axis=1), "narrow", 0)
    kept_coeffs = jnp.take(coeffs_in, keep_order, axis=1)
    kept_stats = jnp.take(stats_in, keep_order, axis=1)
    at_front = member == 0
    whole_coeffs = jnp.concatenate(
        [
            jnp.where(at_front, kept_coeffs, returned_coeffs),
            jnp.where(at_front, returned_coeffs, kept_coeffs),
        ],
        axis=2,
    )
    whole_stats = jnp.concatenate(
        [
            jnp.where(at_front, kept_stats, returned_stats),
            jnp.where(at_front, returned_stats, kept_stats),
        ],
        axis=2,
    )
    through = jnp.argsort(jnp.take(arrived_tags, keep_order) // 2 * block_count + position)
    relayed_coeffs = jnp.take(whole_coeffs, through, axis=1)
    relayed_stats = jnp.take(whole_stats, through, axis=1)
    new_coeffs = lax.all_to_all(relayed_coeffs, "narrow", split_axis=1, concat_axis=1, tiled=True)
    new_stats = lax.all_to_all(relayed_stats, "narrow", split_axis=1, concat_axis=1, tiled=True)
    flat_stats = new_stats.reshape(7, elem_count)
    return (new_coeffs.reshape(coeff_count, elem_count), flat_stats[:6], flat_stats[6])


def solution(mesh):
    return jax.shard_map(
        per_device,
        mesh=mesh,
        in_specs=(
            P(None, ("wide", "narrow")),
            P(None, ("wide", "narrow")),
            P(("wide", "narrow"), None, None),
            P(),
            P(("wide", "narrow")),
            P(("wide", "narrow")),
        ),
        out_specs=(P(None, ("wide", "narrow")), P(None, ("wide", "narrow")), P(("wide", "narrow"))),
        check_vma=False,
    )
```

profile of v0, /device:TPU:24, one launch (start us, length us, event | category | flops | bytes accessed | tf_op | source)
XLA Modules:
  0.0 321.3 jit_solution(11149431525572227855)
XLA Ops:
  0.6 1.0 slice_reduce_fusion.3
  1.7 1.6 copy.50
  3.4 0.7 copy.53
  4.7 2.0 collective-permute-start.3
  6.8 0.6 gather_fusion.10
  7.4 3.6 %collective-permute-start.4 = (bf16[100,2,128]{2,0,1:T(8,128)(2,1)S(1)}, bf16[100,2,128]{2,0,1:T(8,128)(2,1)S(1)}, u32[]{:S(2)}, u32[]{:S(2)}) collective-permute-start(bf16[100,2,128]{2,0,1:T(8,128)(2,1)S(1)} %select_bitcast_fusion.6), channel_id=1, source_target_pairs={{0,508},{4,0},{8,4},{12,8},{16,12},{20,16},{24,20},{28,24},{32,28}... | collective-permute-start | bytes 153608 | tf_op jit(solution)/shard_map/ppermute | solution.py:10
  11.7 3.4 %collective-permute-start.5 = (bf16[100,2,128]{2,0,1:T(8,128)(2,1)S(1)}, bf16[100,2,128]{2,0,1:T(8,128)(2,1)S(1)}, u32[]{:S(2)}, u32[]{:S(2)}) collective-permute-start(bf16[100,2,128]{2,0,1:T(8,128)(2,1)S(1)} %select_bitcast_fusion.5), channel_id=1, source_target_pairs={{0,1},{1,2},{2,3},{3,0},{4,5},{5,6},{6,7},{7,4},{8,9},{9,10},{10,1... | collective-permute-start | bytes 153608 | tf_op jit(solution)/shard_map/ppermute | solution.py:10
  15.8 3.6 %collective-permute-start.6 = (bf16[100,2,128]{2,0,1:T(8,128)(2,1)S(1)}, bf16[100,2,128]{2,0,1:T(8,128)(2,1)S(1)}, u32[]{:S(2)}, u32[]{:S(2)}) collective-permute-start(bf16[100,2,128]{2,0,1:T(8,128)(2,1)S(1)} %select_bitcast_fusion.4), channel_id=1, source_target_pairs={{0,3},{1,0},{2,1},{3,2},{4,7},{5,4},{6,5},{7,6},{8,11},{9,8},{10,9... | collective-permute-start | bytes 153608 | tf_op jit(solution)/shard_map/ppermute | solution.py:10
  19.7 2.2 collective-permute-start
  22.8 1.4 fusion.28
  24.3 0.6 convert_element_type.36
  24.9 1.2 gather_fusion.3
  26.4 1.2 gather_fusion.4
  28.7 14.9 %gather_fusion.13 = bf16[4096,100]{1,0:T(8,128)(2,1)} fusion(bf16[100,5120]{0,1:T(8,128)(2,1)S(1)} %pad_maximum_fusion, s32[4096]{0:T(1024)S(1)} %fusion.38), kind=kCustom, calls=%fused_computation.4.clone | custom fusion | bytes 1654784 | tf_op jit(solution)/shard_map/jit(_take)/gather | solution.py:86
  43.6 14.9 %gather_fusion.14 = bf16[4096,100]{1,0:T(8,128)(2,1)} fusion(bf16[100,5120]{0,1:T(8,128)(2,1)S(1)} %pad_maximum_fusion, s32[4096]{0:T(1024)S(1)} %fusion.39), kind=kCustom, calls=%fused_computation.13.clone | custom fusion | bytes 1654784 | tf_op jit(solution)/shard_map/jit(_take)/gather | solution.py:86
  58.4 14.9 %gather_fusion.15 = bf16[4096,100]{1,0:T(8,128)(2,1)} fusion(bf16[100,5120]{0,1:T(8,128)(2,1)S(1)} %pad_maximum_fusion, s32[4096]{0:T(1024)S(1)} %fusion.40), kind=kCustom, calls=%fused_computation.14.clone | custom fusion | bytes 1654784 | tf_op jit(solution)/shard_map/jit(_take)/gather | solution.py:86
  73.3 12.1 %gather_fusion.16 = bf16[4096,100]{1,0:T(8,128)(2,1)S(1)} fusion(bf16[100,5120]{0,1:T(8,128)(2,1)S(1)} %pad_maximum_fusion, s32[4096]{0:T(1024)S(1)} %fusion.41), kind=kCustom, calls=%fused_computation.15.clone | custom fusion | bytes 1654784 | tf_op jit(solution)/shard_map/jit(_take)/gather | solution.py:86
  85.5 2.5 fusion.3
  88.0 0.8 fusion.2
  89.3 0.8 fusion.1
  90.1 0.8 fusion
  90.9 1.7 reshape.171
  92.6 4.4 %multiply_reduce_fusion = (f32[4096]{0:T(1024)S(1)}, f32[4096]{0:T(1024)S(1)}, f32[4096]{0:T(1024)S(1)}, f32[4096]{0:T(1024)S(1)}, f32[4096]{0:T(1024)S(1)}, /*index=5*/f32[4096]{0:T(1024)S(1)}) fusion(f32[25,3,4096]{2,1,0:T(4,128)} %reshape.171), kind=kLoop, calls=%fused_computation.56 | loop fusion | flops 1204224 | bytes 1327104 | tf_op jit(solution)/shard_map/reduce_sum | solution.py:30
  97.5 3.7 %collective-permute-start.7 = (f32[7,32,64]{2,0,1:T(8,128)S(1)}, f32[7,32,64]{2,0,1:T(8,128)S(1)}, u32[]{:S(2)}, u32[]{:S(2)}) collective-permute-start(f32[7,32,64]{2,0,1:T(8,128)S(1)} %get-tuple-element.43), channel_id=1, source_target_pairs={{0,1},{1,0},{2,3},{3,2},{4,5},{5,4},{6,7},{7,6},{8,9},{9,8},{10,11... | collective-permute-start | bytes 172040 | tf_op jit(solution)/shard_map/ppermute | solution.py:14
  101.2 0.7 copy.49
  101.9 20.0 %all-to-all-start = ((f32[1,128,1]{2,0,1:T(1,128)}), f32[1,128,1]{2,0,1:T(1,128)S(1)}, u32[]{:S(2)}, u32[]{:S(2)}) async-start(f32[1,128,1]{2,0,1:T(1,128)} %copy.49), calls=%async_computation | async-start | bytes 131072 | tf_op jit(solution)/shard_map/all_to_all | solution.py:143
  121.9 0.8 gather_fusion.17
  122.7 0.8 gather_fusion.18
  123.5 0.8 fusion.56
  124.3 1.1 reshape.403
  125.4 10.2 %all-to-all-done = f32[1,128,1]{2,0,1:T(1,128)S(1)} async-done(((f32[1,128,1]{2,0,1:T(1,128)}), f32[1,128,1]{2,0,1:T(1,128)S(1)}, u32[]{:S(2)}, u32[]{:S(2)}) %all-to-all-start) | async-done | bytes 544 | tf_op jit(solution)/shard_map/all_to_all | solution.py:143
  135.6 6.9 %all-to-all-start.3 = ((f32[128,1,448]{2,1,0:T(1,128)}), f32[128,1,448]{2,1,0:T(1,128)S(1)}, u32[]{:S(2)}, u32[]{:S(2)}) async-start(f32[128,1,448]{2,1,0:T(1,128)} %reshape.403), calls=%async_computation.3 | async-start | bytes 524288 | tf_op jit(solution)/shard_map/all_to_all | solution.py:142
  142.5 0.9 constant_dynamic-slice_fusion.1
  143.3 2.2 collective-permute-start.1
  145.5 1.0 gather_fusion.5
  146.5 12.9 %collective-permute-done.1 = bf16[100,32,64]{0,2,1:T(8,128)(2,1)S(1)} collective-permute-done((bf16[100,32,64]{0,2,1:T(8,128)(2,1)}, bf16[100,32,64]{0,2,1:T(8,128)(2,1)S(1)}, u32[]{:S(2)}, u32[]{:S(2)}) %collective-permute-start.1) | collective-permute-done | bytes 409632 | tf_op jit(solution)/shard_map/ppermute | solution.py:14
  159.4 2.2 gather_fusion.6
  161.6 3.3 %fusion.4 = bf16[100,128,64]{0,2,1:T(8,128)(2,1)} fusion(bf16[128,100,64]{1,2,0:T(8,128)(2,1)} %gather_fusion.6, bf16[128,100,64]{1,2,0:T(8,128)(2,1)S(1)} %gather_fusion.5, pred[128]{0:T(512)(128)(4,1)S(1)} %compare_and_fusion.9, pred[128]{0:T(512)(128)(4,1)S(1)} %copy-done.7, pred[128]{0:T(512)(128)(4,1)S(1)} %copy-done.6, pred[128]{0:T(512)(128)(4,1)S(1)} %fusion.36), kind=kLoop, calls=%fused_computation.30 | loop fusion | flops 3276800 | bytes 4915712 | tf_op jit(solution)/shard_map/jit(_where)/select_n | solution.py:124
  164.9 16.2 %all-to-all-start.1 = ((bf16[100,128,64]{0,2,1:T(8,128)(2,1)}), bf16[100,128,64]{0,2,1:T(8,128)(2,1)S(1)}, u32[]{:S(2)}, u32[]{:S(2)}) async-start(bf16[100,128,64]{0,2,1:T(8,128)(2,1)} %fusion.4), calls=%async_computation.1 | async-start | bytes 4194304 | tf_op jit(solution)/shard_map/all_to_all | solution.py:147
  181.1 2.4 convert_reduce_fusion
  183.4 2.5 sort.48
  186.0 0.7 gather_fusion
  186.7 2.5 sort.50
  189.3 1.6 sort.49
  191.4 1.3 reduce.16
  192.8 0.6 gather_fusion.20
  193.5 2.2 collective-permute-start.8
  195.8 0.6 gather_fusion.19
  196.3 4.6 %collective-permute-done.8 = f32[7,32,64]{2,0,1:T(8,128)S(1)} collective-permute-done((f32[7,32,64]{2,0,1:T(8,128)S(1)}, f32[7,32,64]{2,0,1:T(8,128)S(1)}, u32[]{:S(2)}, u32[]{:S(2)}) %collective-permute-start.8) | collective-permute-done | bytes 57376 | tf_op jit(solution)/shard_map/ppermute | solution.py:14
  201.1 76.9 %all-to-all-done.1 = bf16[100,128,64]{0,2,1:T(8,128)(2,1)S(1)} async-done(((bf16[100,128,64]{0,2,1:T(8,128)(2,1)}), bf16[100,128,64]{0,2,1:T(8,128)(2,1)S(1)}, u32[]{:S(2)}, u32[]{:S(2)}) %all-to-all-start.1) | async-done | bytes 1638432 | tf_op jit(solution)/shard_map/all_to_all | solution.py:147
  278.0 0.6 gather_fusion.8
  278.8 2.2 collective-permute-start.2
  281.1 0.6 gather_fusion.2
  281.8 16.0 %all_to_all.29 = f32[7,32,128]{2,0,1:T(8,128)S(1)} all-to-all(f32[7,32,128]{2,0,1:T(8,128)S(1)} %select_bitcast_fusion.3), channel_id=1, replica_groups=mesh['wide'=128,'narrow'=4] {'narrow'}, dimensions={1} | all-to-all | bytes 229376 | tf_op jit(solution)/shard_map/all_to_all | solution.py:177
  297.8 0.6 slice.143
  298.4 0.6 gather_fusion.7
  299.0 1.2 bitcast_select_fusion.3
  300.5 0.7 copy.51
  301.2 0.7 gather_fusion.1
  301.9 1.0 select_bitcast_fusion
  303.0 3.5 %all-to-all-start.2 = ((bf16[100,32,128]{2,0,1:T(8,128)(2,1)}), bf16[100,32,128]{2,0,1:T(8,128)(2,1)S(1)}, u32[]{:S(2)}, u32[]{:S(2)}) async-start(bf16[100,32,128]{2,0,1:T(8,128)(2,1)} %select_bitcast_fusion), calls=%async_computation.2 | async-start | bytes 1703936 | tf_op jit(solution)/shard_map/all_to_all | solution.py:176
  306.5 0.7 slice_bitcast_fusion
  307.1 12.8 %all-to-all-done.2 = bf16[100,32,128]{2,0,1:T(8,128)(2,1)S(1)} async-done(((bf16[100,32,128]{2,0,1:T(8,128)(2,1)}), bf16[100,32,128]{2,0,1:T(8,128)(2,1)S(1)}, u32[]{:S(2)}, u32[]{:S(2)}) %all-to-all-start.2) | async-done | bytes 819232 | tf_op jit(solution)/shard_map/all_to_all | solution.py:176
  320.1 1.2 copy.62
  (109 shorter events, 6.9 us)
Async XLA Ops:
  3.3 16.2 %copy-start.12 = (s32[32]{0:T(128)S(1)}, s32[32]{0:T(128)}, u32[]{:S(2)}) copy-start(s32[32]{0:T(128)} %param.24) | copy-start | bytes 388
  3.3 18.6 %copy-start.4 = (s32[4,4096]{1,0:T(4,128)S(1)}, s32[4,4096]{1,0:T(4,128)}, u32[]{:S(2)}) copy-start(s32[4,4096]{1,0:T(4,128)} %param.21) | copy-start | bytes 196612
  3.3 19.5 %copy-start.2 = (bf16[100,4096]{1,0:T(8,128)(2,1)S(1)}, bf16[100,4096]{1,0:T(8,128)(2,1)}, u32[]{:S(2)}) copy-start(bf16[100,4096]{1,0:T(8,128)(2,1)} %param.20) | copy-start | bytes 2457604
  3.3 19.5 %copy-start.3 = (bf16[5,75,100]{2,1,0:T(8,128)(2,1)S(1)}, bf16[5,75,100]{2,1,0:T(8,128)(2,1)}, u32[]{:S(2)}) copy-start(bf16[5,75,100]{2,1,0:T(8,128)(2,1)} %param.23) | copy-start | bytes 225004
  4.7 19.6 %copy-start.13 = (s32[32]{0:T(128)S(1)}, s32[32]{0:T(128)}, u32[]{:S(2)}) copy-start(s32[32]{0:T(128)} %param.25) | copy-start | bytes 388
  4.7 23.4 %collective-permute-start.3 = (bf16[100,2,128]{2,0,1:T(8,128)(2,1)S(1)}, bf16[100,2,128]{2,0,1:T(8,128)(2,1)S(1)}, u32[]{:S(2)}, u32[]{:S(2)}) collective-permute-start(bf16[100,2,128]{2,0,1:T(8,128)(2,1)S(1)} %select_bitcast_fusion.7), channel_id=1, source_target_pairs={{0,4},{4,8},{8,12},{12,16},{16,20},{20,24},{24,28},{28,32},{32,36}... | collective-permute-start | bytes 153608 | tf_op jit(solution)/shard_map/ppermute | solution.py:10
  7.4 20.7 %collective-permute-start.4 = (bf16[100,2,128]{2,0,1:T(8,128)(2,1)S(1)}, bf16[100,2,128]{2,0,1:T(8,128)(2,1)S(1)}, u32[]{:S(2)}, u32[]{:S(2)}) collective-permute-start(bf16[100,2,128]{2,0,1:T(8,128)(2,1)S(1)} %select_bitcast_fusion.6), channel_id=1, source_target_pairs={{0,508},{4,0},{8,4},{12,8},{16,12},{20,16},{24,20},{28,24},{32,28}... | collective-permute-start | bytes 153608 | tf_op jit(solution)/shard_map/ppermute | solution.py:10
  11.7 16.4 %collective-permute-start.5 = (bf16[100,2,128]{2,0,1:T(8,128)(2,1)S(1)}, bf16[100,2,128]{2,0,1:T(8,128)(2,1)S(1)}, u32[]{:S(2)}, u32[]{:S(2)}) collective-permute-start(bf16[100,2,128]{2,0,1:T(8,128)(2,1)S(1)} %select_bitcast_fusion.5), channel_id=1, source_target_pairs={{0,1},{1,2},{2,3},{3,0},{4,5},{5,6},{6,7},{7,4},{8,9},{9,10},{10,1... | collective-permute-start | bytes 153608 | tf_op jit(solution)/shard_map/ppermute | solution.py:10
  15.8 12.3 %collective-permute-start.6 = (bf16[100,2,128]{2,0,1:T(8,128)(2,1)S(1)}, bf16[100,2,128]{2,0,1:T(8,128)(2,1)S(1)}, u32[]{:S(2)}, u32[]{:S(2)}) collective-permute-start(bf16[100,2,128]{2,0,1:T(8,128)(2,1)S(1)} %select_bitcast_fusion.4), channel_id=1, source_target_pairs={{0,3},{1,0},{2,1},{3,2},{4,7},{5,4},{6,5},{7,6},{8,11},{9,8},{10,9... | collective-permute-start | bytes 153608 | tf_op jit(solution)/shard_map/ppermute | solution.py:10
  19.7 6.4 %collective-permute-start = (f32[2,32]{1,0:T(2,128)S(1)}, f32[2,32]{1,0:T(2,128)S(1)}, u32[]{:S(2)}, u32[]{:S(2)}) collective-permute-start(f32[2,32]{1,0:T(2,128)S(1)} %add_convert_fusion), channel_id=1, source_target_pairs={{0,1},{1,0},{2,3},{3,2},{4,5},{5,4},{6,7},{7,6},{8,9},{9,8},{10,11... | collective-permute-start | bytes 776 | tf_op jit(solution)/shard_map/ppermute | solution.py:14
  26.2 2.4 copy-start.10
  26.3 2.3 copy-start.5
  85.5 2.5 copy-start.1
  88.0 1.2 copy-start
  90.9 6.1 %copy-start.9 = (f32[32]{0:T(128)S(1)}, f32[32]{0:T(128)}, u32[]{:S(2)}) copy-start(f32[32]{0:T(128)} %convert_element_type.36) | copy-start | bytes 388
  92.6 8.5 %copy-start.11 = (s32[128]{0:T(128)S(1)}, s32[128]{0:T(128)}, u32[]{:S(2)}) copy-start(s32[128]{0:T(128)} %copy-done.10) | copy-start | bytes 1540
  92.6 8.5 %copy-start.8 = (f32[1,128,1]{1,2,0:T(1,128)S(1)}, f32[1,128,1]{1,2,0:T(1,128)}, u32[]{:S(2)}) copy-start(f32[1,128,1]{1,2,0:T(1,128)} %convert_bitcast_fusion) | copy-start | bytes 1540
  97.0 26.5 %copy-start.6 = (pred[128]{0:T(512)(128)(4,1)S(1)}, pred[128]{0:T(512)(128)(4,1)}, u32[]{:S(2)}) copy-start(pred[128]{0:T(512)(128)(4,1)} %copy-done.5) | copy-start | bytes 388
  97.0 26.5 %copy-start.7 = (pred[128]{0:T(512)(128)(4,1)S(1)}, pred[128]{0:T(512)(128)(4,1)}, u32[]{:S(2)}) copy-start(pred[128]{0:T(512)(128)(4,1)} %compare_and_fusion.10) | copy-start | bytes 388
  97.5 25.2 %collective-permute-start.7 = (f32[7,32,64]{2,0,1:T(8,128)S(1)}, f32[7,32,64]{2,0,1:T(8,128)S(1)}, u32[]{:S(2)}, u32[]{:S(2)}) collective-permute-start(f32[7,32,64]{2,0,1:T(8,128)S(1)} %get-tuple-element.43), channel_id=1, source_target_pairs={{0,1},{1,0},{2,3},{3,2},{4,5},{5,4},{6,7},{7,6},{8,9},{9,8},{10,11... | collective-permute-start | bytes 172040 | tf_op jit(solution)/shard_map/ppermute | solution.py:14
  101.9 33.7 %all-to-all-start = ((f32[1,128,1]{2,0,1:T(1,128)}), f32[1,128,1]{2,0,1:T(1,128)S(1)}, u32[]{:S(2)}, u32[]{:S(2)}) async-start(f32[1,128,1]{2,0,1:T(1,128)} %copy.49), calls=%async_computation | async-start | bytes 131072 | tf_op jit(solution)/shard_map/all_to_all | solution.py:143
  135.6 29.3 %all-to-all-start.3 = ((f32[128,1,448]{2,1,0:T(1,128)}), f32[128,1,448]{2,1,0:T(1,128)S(1)}, u32[]{:S(2)}, u32[]{:S(2)}) async-start(f32[128,1,448]{2,1,0:T(1,128)} %reshape.403), calls=%async_computation.3 | async-start | bytes 524288 | tf_op jit(solution)/shard_map/all_to_all | solution.py:142
  143.3 16.1 %collective-permute-start.1 = (bf16[100,32,64]{0,2,1:T(8,128)(2,1)}, bf16[100,32,64]{0,2,1:T(8,128)(2,1)S(1)}, u32[]{:S(2)}, u32[]{:S(2)}) collective-permute-start(bf16[100,32,64]{0,2,1:T(8,128)(2,1)} %get-tuple-element.39), channel_id=1, source_target_pairs={{0,1},{1,0},{2,3},{3,2},{4,5},{5,4},{6,7},{7,6},{8,9},{9,8},{10,11... | collective-permute-start | bytes 1228808 | tf_op jit(solution)/shard_map/ppermute | solution.py:14
  164.9 113.1 %all-to-all-start.1 = ((bf16[100,128,64]{0,2,1:T(8,128)(2,1)}), bf16[100,128,64]{0,2,1:T(8,128)(2,1)S(1)}, u32[]{:S(2)}, u32[]{:S(2)}) async-start(bf16[100,128,64]{0,2,1:T(8,128)(2,1)} %fusion.4), calls=%async_computation.1 | async-start | bytes 4194304 | tf_op jit(solution)/shard_map/all_to_all | solution.py:147
  193.5 7.4 %collective-permute-start.8 = (f32[7,32,64]{2,0,1:T(8,128)S(1)}, f32[7,32,64]{2,0,1:T(8,128)S(1)}, u32[]{:S(2)}, u32[]{:S(2)}) collective-permute-start(f32[7,32,64]{2,0,1:T(8,128)S(1)} %select_bitcast_fusion.2), channel_id=1, source_target_pairs={{0,1},{1,0},{2,3},{3,2},{4,5},{5,4},{6,7},{7,6},{8,9},{9,8},{10,11... | collective-permute-start | bytes 172040 | tf_op jit(solution)/shard_map/ppermute | solution.py:14
  278.8 20.3 %collective-permute-start.2 = (bf16[100,32,64]{0,2,1:T(8,128)(2,1)S(1)}, bf16[100,32,64]{0,2,1:T(8,128)(2,1)}, u32[]{:S(2)}, u32[]{:S(2)}) collective-permute-start(bf16[100,32,64]{0,2,1:T(8,128)(2,1)S(1)} %select_bitcast_fusion.1), channel_id=1, source_target_pairs={{0,1},{1,0},{2,3},{3,2},{4,5},{5,4},{6,7},{7,6},{8,9},{9,8},{10,11... | collective-permute-start | bytes 1228808 | tf_op jit(solution)/shard_map/ppermute | solution.py:14
  303.0 16.9 %all-to-all-start.2 = ((bf16[100,32,128]{2,0,1:T(8,128)(2,1)}), bf16[100,32,128]{2,0,1:T(8,128)(2,1)S(1)}, u32[]{:S(2)}, u32[]{:S(2)}) async-start(bf16[100,32,128]{2,0,1:T(8,128)(2,1)} %select_bitcast_fusion), calls=%async_computation.2 | async-start | bytes 1703936 | tf_op jit(solution)/shard_map/all_to_all | solution.py:176
where the time goes:
time: 323 us; the launch traced here: 321 us
  waiting for transfers between devices  117 us (36%)
  local copies, waits for them, and re-layouts  83.2 us (26%)
  starting transfers between devices  71.7 us (22%)
  other arithmetic  25.1 us (8%)
  blocking collectives  16 us (5%)
  matrix products  6.45 us (2%)
    all_to_all x1, waiting for transfers between devices, per_device(): lax.all_to_all(joined_coeffs, 'wide', split_axis=1, concat_axis=1, tiled=...  76.9 us
    gather x4, local copies, waits for them, and re-layouts, per_device(): gathered = jnp.take(extended, neighbours[face_index], axis=1)  56.8 us
    all_to_all x1, starting transfers between devices, per_device(): lax.all_to_all(pair_tags.astype(jnp.float32)[None, :], 'wide', split_axis...  20 us
    ppermute x5, waiting for transfers between devices, swapped(): lax.ppermute(value, axis, [(i, i ^ 1 << apart) for i in range(lax.axis_si...  17.6 us
    all_to_all x1, starting transfers between devices, per_device(): lax.all_to_all(joined_coeffs, 'wide', split_axis=1, concat_axis=1, tiled=...  16.2 us
    all_to_all x1, blocking collectives, per_device(): lax.all_to_all(relayed_stats, 'narrow', split_axis=1, concat_axis=1, tile...  16 us
    all_to_all x1, waiting for transfers between devices, per_device(): lax.all_to_all(relayed_coeffs, 'narrow', split_axis=1, concat_axis=1, til...  12.8 us
    ppermute x4, starting transfers between devices, passed_along(): return lax.ppermute(value, axis, pairs)  12.7 us
  transfers between devices with their start and end apart: 13, of which 5 were waited for; matrix products, arithmetic and copies ran while one was open for 11% of the time, Pallas kernels for 0%

commit v1 on v0

v1 whole, which is shorter than its diff:
```python
import jax
import jax.numpy as jnp
from jax import lax
from jax.experimental import pallas as pl
from jax.experimental.pallas import tpu as pltpu
from jax.sharding import PartitionSpec as P

MESH = pl.DeviceIdType.MESH
WIDE = 128
NARROW = 4
BLK = 128
BLOCKS = 32
ELEMS = BLK * BLOCKS
COEF = 100
HALO = 8 * BLK
EXT = ELEMS + HALO
HALF = 16 * BLK
CODE = 1024

INFO, SWAP_A, SWAP_B, SWAP_C, HALO_UP, HALO_DOWN, HALO_LEFT, HALO_RIGHT = range(8)
WIDE_TAG, WIDE_A, WIDE_B, SWAP_L, WIDE_L, NARROW_C, NARROW_A, NARROW_B, NARROW_L = range(8, 17)
GROUPS = 17


def aligned(value, step):
    return pl.multiple_of(value, step)


def kernel(
    coef, nbr, halo, wts, info, modal, metric, work,
    tiles, pair_a, pair_b, pair_c, late, pinfo, both, pick_v, pick_s, tab_v, tab_s, cnt_v, cnt_r, cnt_s,
    hsend, hrecv, tags, tags2, send_a, recv_a, send_b, recv_b, send_l, recv_l,
    out_a, out_b, out_l, last, table, own, rows, sent, came, local,
):
    w = lax.axis_index("wide")
    a = lax.axis_index("narrow")
    h = lax.rem(a, 2)
    j = a // 2
    partner = a + 1 - 2 * h
    mine = pl.ds(h * BLOCKS, BLOCKS)
    pairs = (pair_a, pair_b, pair_c)

    def remote(src, dst, group, wide, narrow):
        return pltpu.make_async_remote_copy(
            src_ref=src, dst_ref=dst, send_sem=sent.at[group], recv_sem=came.at[group],
            device_id=(wide, narrow), device_id_type=MESH,
        )

    def wait_bytes(ref, sem):
        pltpu.make_async_copy(ref, ref, sem).wait()

    barrier = pltpu.get_barrier_semaphore()

    def greet(i, carry):
        pl.semaphore_signal(barrier, inc=1, device_id=(lax.rem(w + i, WIDE), a), device_id_type=MESH)
        return carry

    for d in range(1, NARROW):
        pl.semaphore_signal(barrier, inc=1, device_id=(w, lax.rem(a + d, NARROW)), device_id_type=MESH)
    lax.fori_loop(1, WIDE, greet, 0)
    pl.semaphore_wait(barrier, WIDE - 1 + NARROW - 1)

    swap_info = remote(info, pinfo, INFO, w, partner)
    swap_info.start()

    def retile(b, carry):
        at = pl.ds(aligned(b * BLK, BLK), BLK)
        for k in range(6):
            tiles[k, b] = coef[16 * k : 16 * k + 16, at]
        end = coef[96:100, at]
        tiles[6, b] = jnp.concatenate([end, jnp.zeros((12, BLK), end.dtype)], axis=0)
        return carry

    lax.fori_loop(0, BLOCKS, retile, 0)
    swaps = []
    for k in range(3):
        swap = remote(tiles.at[3 * (1 - h) + k], pairs[k].at[mine], SWAP_A + k, w, partner)
        swap.start()
        swaps.append(swap)

    places = [
        (lax.rem(w + WIDE - 1, WIDE), a),
        (lax.rem(w + 1, WIDE), a),
        (w, lax.rem(a + NARROW - 1, NARROW)),
        (w, lax.rem(a + 1, NARROW)),
    ]
    halos = []
    for k in range(4):
        for s in range(2):
            block = halo[k * 2 + s]
            for r in range(7):
                hsend[k, s, r] = tiles[r, block]
        push = remote(hsend.at[k], hrecv.at[k ^ 1], HALO_UP + k, *places[k])
        push.start()
        halos.append(push)

    def keep(b, carry):
        for k in range(3):
            pairs[k][h * BLOCKS + b] = tiles[3 * h + k, b]
        return carry

    lax.fori_loop(0, BLOCKS, keep, 0)

    swap_info.wait()
    both[...] = info[...] + pinfo[...]
    entries = jnp.transpose(jnp.broadcast_to(both[...], (BLK, BLK)))
    lane = lax.broadcasted_iota(jnp.int32, (BLK, BLK), 1)
    sub = lax.broadcasted_iota(jnp.int32, (BLK, BLK), 0)
    goes = (entries >= CODE) & ((entries & (CODE - 1)) // NARROW == lane)
    pick = jnp.sum(jnp.where(goes, sub, 0), axis=0, keepdims=True)
    pick_v[...] = jnp.broadcast_to(pick, (8, BLK))
    to_scalar = pltpu.make_async_copy(pick_v, pick_s, local.at[0])
    to_scalar.start()
    to_scalar.wait()

    def spread(src, dst, group):
        def one(i, carry):
            t = lax.rem(w + i, WIDE)
            remote(src.at[t], dst.at[w], group, t, a).start()
            return carry

        lax.fori_loop(1, WIDE, one, 0)

    swaps[0].wait()

    def pack_a(t, carry):
        send_a[t] = pair_a[pick_s[0, t]]
        return carry

    lax.fori_loop(0, WIDE, pack_a, 0)
    recv_a[w] = send_a[w]
    spread(send_a, recv_a, WIDE_A)

    swaps[1].wait()
    swaps[2].wait()

    def pack_b(t, carry):
        send_b[t, 0:16] = pair_b[pick_s[0, t]]
        send_b[t, 16:32] = pair_c[pick_s[0, t]]
        return carry

    lax.fori_loop(0, WIDE, pack_b, 0)
    recv_b[w] = send_b[w]
    spread(send_b, recv_b, WIDE_B)

    def one_tag(i, carry):
        remote(both, tags.at[w], WIDE_TAG, lax.rem(w + i, WIDE), a).start()
        return carry

    tags[w] = both[...]
    lax.fori_loop(1, WIDE, one_tag, 0)

    def product(cols, weights):
        return lax.dot_general(
            cols, weights, (((0,), (0,)), ((), ())), preferred_element_type=jnp.float32
        )

    def own_block(b, carry):
        at = pl.ds(aligned(b * BLK, BLK), BLK)
        result = product(coef[:, at], wts[...])
        own[at, :] = result[:, :BLK]
        for f in range(4):
            table[f, at, :] = result[:, (f + 1) * BLK : (f + 2) * BLK]
        return carry

    lax.fori_loop(0, BLOCKS, own_block, 0)
    for push in halos:
        push.wait()
    for k in range(4):
        for s in range(2):
            result = product(hrecv[k, s].reshape(112, BLK)[:COEF], wts[:, BLK:])
            first = ELEMS + (2 * k + s) * BLK
            for f in range(4):
                table[f, first : first + BLK, :] = result[:, f * BLK : (f + 1) * BLK]

    def gather(i, carry):
        for u in range(8):
            e = i * 8 + u
            total = table[0, nbr[0, e]]
            for f in range(1, 4):
                total = total + table[f, nbr[f, e]]
            rows[e] = total
        return carry

    lax.fori_loop(0, ELEMS // 8, gather, 0)

    def metric_block(b, carry):
        at = pl.ds(aligned(b * BLK, BLK), BLK)
        derivs = jnp.transpose(own[at, :] + rows[at, :])
        x, y, z = derivs[0:32], derivs[32:64], derivs[64:96]

        def mean(left, right, base):
            return base + jnp.sum(left * right, axis=0, keepdims=True) * (1.0 / 25)

        full = jnp.concatenate(
            [mean(x, x, 1.0), mean(y, y, 1.0), mean(z, z, 1.0), mean(x, y, 0.0), mean(x, z, 0.0), mean(y, z, 0.0)],
            axis=0,
        )
        high = full.astype(jnp.bfloat16).astype(jnp.float32)
        tail = coef[96:100, at].astype(jnp.float32)
        tile = jnp.concatenate([high, tail[0:2], full - high, tail[2:4]], axis=0)
        late[h * BLOCKS + b] = tile.astype(jnp.bfloat16)
        return carry

    lax.fori_loop(0, BLOCKS, metric_block, 0)

    swap_late = remote(late.at[mine], late.at[mine], SWAP_L, w, partner)
    swap_late.start()
    swap_late.wait()
    odd = lax.rem(w + h, 2)

    def pack_l(i, carry):
        t = 2 * i + h
        send_l[t] = late[pick_s[0, t]]
        return carry

    lax.fori_loop(0, WIDE // 2, pack_l, 0)

    def send_late(i, carry):
        t = lax.rem(w + 2 * i + odd, WIDE)
        remote(send_l.at[t], recv_l.at[w], WIDE_L, t, a).start()
        return carry

    @pl.when(odd == 0)
    def _():
        recv_l[w] = send_l[w]

    lax.fori_loop(1 - odd, WIDE // 2, send_late, 0)

    wait_bytes(tags.at[pl.ds(0, WIDE - 1)], came.at[WIDE_TAG])

    def flat(i, carry):
        tags2[pl.ds(i, 1), :] = tags[i]
        return carry

    lax.fori_loop(0, WIDE, flat, 0)
    codes = jnp.transpose(tags2[...])
    here = (codes >= CODE) & ((codes & (CODE - 1)) // NARROW == w)
    kinds = jnp.where(here, (sub // BLOCKS) * NARROW + lax.rem(codes, NARROW) + 1, 0)
    kind = jnp.sum(kinds, axis=0, keepdims=True) - 1
    count = jnp.sum(jnp.where(here, codes // CODE, 0), axis=0, keepdims=True)
    lane8 = lax.broadcasted_iota(jnp.int32, (8, BLK), 1)
    sub8 = lax.broadcasted_iota(jnp.int32, (8, BLK), 0)
    chosen = (jnp.broadcast_to(kind, (8, BLK)) == sub8).astype(jnp.int32)
    rank = chosen
    for step in (1, 2, 4, 8, 16, 32, 64):
        rank = rank + jnp.where(lane8 >= step, pltpu.roll(rank, step, 1), 0)
    rank = rank - chosen
    counts = jnp.broadcast_to(count, (8, BLK))
    froms = jnp.zeros((8, BLK), jnp.int32)
    works = jnp.zeros((8, BLK), jnp.int32)
    for r in range(8):
        found = (chosen > 0) & (rank == r)
        froms = jnp.where(
            lane8 == r, jnp.sum(jnp.where(found, lane8, 0), axis=1, keepdims=True), froms
        )
        works = jnp.where(
            lane8 == r, jnp.sum(jnp.where(found, counts, 0), axis=1, keepdims=True), works
        )
    tab_v[...] = froms
    cnt_v[...] = works
    to_scalar = pltpu.make_async_copy(tab_v, tab_s, local.at[1])
    to_scalar.start()
    to_scalar.wait()
    cnt_r[a] = cnt_v[...]
    for d in range(1, NARROW):
        remote(cnt_v, cnt_r.at[a], NARROW_C, w, lax.rem(a + d, NARROW)).start()

    def collect(src, dst):
        def one(s, carry):
            at = pl.ds(aligned(s * BLK, BLK), BLK)
            for c in range(NARROW):
                dst[c, :, at] = src[tab_s[(s // 8) * NARROW + c, lax.rem(s, 8)]]
            return carry

        lax.fori_loop(0, 16, one, 0)

    side = pl.ds(aligned(j * HALF, HALF), HALF)

    def deliver(src, recv, out, first, tall, group):
        wait_bytes(recv.at[pl.ds(0, WIDE - 1)], came.at[src])
        collect(recv, out)
        place = pl.ds(aligned(first, 16), tall)
        for d in range(1, NARROW):
            c = lax.rem(a + d, NARROW)
            remote(out.at[c], modal.at[place, side], group, w, c).start()
        modal[place, side] = out[a]

    deliver(WIDE_A, recv_a, out_a, 48 * h, 16, NARROW_A)
    deliver(WIDE_B, recv_b, out_b, 48 * h + 16, 32, NARROW_B)

    @pl.when(odd == 0)
    def _():
        wait_bytes(recv_l.at[pl.ds(0, WIDE - 1)], came.at[WIDE_L])
        collect(recv_l, out_l)
        for d in range(1, NARROW):
            c = lax.rem(a + d, NARROW)
            remote(out_l.at[c], last.at[j], NARROW_L, w, c).start()
        last[j] = out_l[a]

    wait_bytes(cnt_r.at[pl.ds(0, 3)], came.at[NARROW_C])
    to_scalar = pltpu.make_async_copy(cnt_r, cnt_s, local.at[2])
    to_scalar.start()

    @pl.when(odd == 0)
    def _():
        wait_bytes(last.at[0], came.at[NARROW_L])

    @pl.when(odd == 1)
    def _():
        wait_bytes(last, came.at[NARROW_L])

    to_scalar.wait()
    for p in range(2):
        tiles = last[p].astype(jnp.float32)
        full = tiles[0:8] + tiles[8:16]
        metric[:, p * HALF : (p + 1) * HALF] = full[0:6]
        modal[96:100, p * HALF : (p + 1) * HALF] = jnp.concatenate(
            [tiles[6:8], tiles[14:16]], axis=0
        ).astype(jnp.bfloat16)
        xx, yy, zz = full[0:1], full[1:2], full[2:3]
        xy, xz, yz = full[3:4], full[4:5], full[5:6]
        det = xx * (yy * zz - yz * yz) - xy * (xy * zz - yz * xz) + xz * (xy * yz - yy * xz)
        root = jnp.sqrt(det)
        for s in range(16):
            units = cnt_s[2 * p, (s // 8) * NARROW + a, s % 8].astype(jnp.float32)
            first = p * HALF + s * BLK
            work[:, first : first + BLK] = root[:, s * BLK : (s + 1) * BLK] * units

    wait_bytes(out_a.at[pl.ds(0, 3)], came.at[NARROW_A])
    wait_bytes(out_b.at[pl.ds(0, 3)], came.at[NARROW_B])
    wait_bytes(send_a.at[pl.ds(0, WIDE - 1)], sent.at[WIDE_A])
    wait_bytes(send_b.at[pl.ds(0, WIDE - 1)], sent.at[WIDE_B])
    wait_bytes(tags.at[pl.ds(0, WIDE - 1)], sent.at[WIDE_TAG])
    wait_bytes(cnt_r.at[pl.ds(0, 3)], sent.at[NARROW_C])
    wait_bytes(out_a.at[pl.ds(0, 3)], sent.at[NARROW_A])
    wait_bytes(out_b.at[pl.ds(0, 3)], sent.at[NARROW_B])

    @pl.when(odd == 0)
    def _():
        wait_bytes(send_l.at[pl.ds(0, WIDE // 2 - 1)], sent.at[WIDE_L])
        wait_bytes(out_l.at[pl.ds(0, 3)], sent.at[NARROW_L])

    @pl.when(odd == 1)
    def _():
        wait_bytes(send_l.at[pl.ds(0, WIDE // 2)], sent.at[WIDE_L])


def per_device(coefficients, neighbours, halo_blocks, recon_weight, owner_device, work_count):
    member = lax.axis_index("narrow") % 2
    code = jnp.tile(owner_device + CODE * work_count, 4).reshape(1, BLK)
    lane = lax.broadcasted_iota(jnp.int32, (1, BLK), 1)
    info = jnp.where(lane // BLOCKS == member, code, 0)
    weights = recon_weight.reshape(5, 25, 3, COEF).transpose(3, 0, 2, 1)
    weights = jnp.pad(weights, ((0, 0), (0, 0), (0, 1), (0, 7))).reshape(COEF, 5 * BLK)
    vmem = pl.BlockSpec(memory_space=pltpu.VMEM)
    smem = pl.BlockSpec(memory_space=pltpu.SMEM)
    low, full, whole = jnp.bfloat16, jnp.float32, jnp.int32
    modal, metric, work = pl.pallas_call(
        kernel,
        out_shape=(
            jax.ShapeDtypeStruct((COEF, ELEMS), low),
            jax.ShapeDtypeStruct((6, ELEMS), full),
            jax.ShapeDtypeStruct((1, ELEMS), full),
        ),
        in_specs=[vmem, smem, smem, vmem, vmem],
        out_specs=(vmem, vmem, vmem),
        scratch_shapes=[
            pltpu.VMEM((7, BLOCKS, 16, BLK), low),
            pltpu.VMEM((2 * BLOCKS, 16, BLK), low),
            pltpu.VMEM((2 * BLOCKS, 16, BLK), low),
            pltpu.VMEM((2 * BLOCKS, 16, BLK), low),
            pltpu.VMEM((2 * BLOCKS, 16, BLK), low),
            pltpu.VMEM((1, BLK), whole),
            pltpu.VMEM((1, BLK), whole),
            pltpu.VMEM((8, BLK), whole),
            pltpu.SMEM((8, BLK), whole),
            pltpu.VMEM((8, BLK), whole),
            pltpu.SMEM((8, BLK), whole),
            pltpu.VMEM((8, BLK), whole),
            pltpu.VMEM((NARROW, 8, BLK), whole),
            pltpu.SMEM((NARROW, 8, BLK), whole),
            pltpu.VMEM((4, 2, 7, 16, BLK), low),
            pltpu.VMEM((4, 2, 7, 16, BLK), low),
            pltpu.VMEM((WIDE, 1, BLK), whole),
            pltpu.VMEM((WIDE, BLK), whole),
            pltpu.VMEM((WIDE, 16, BLK), low),
            pltpu.VMEM((WIDE, 16, BLK), low),
            pltpu.VMEM((WIDE, 32, BLK), low),
            pltpu.VMEM((WIDE, 32, BLK), low),
            pltpu.VMEM((WIDE, 16, BLK), low),
            pltpu.VMEM((WIDE, 16, BLK), low),
            pltpu.VMEM((NARROW, 16, HALF), low),
            pltpu.VMEM((NARROW, 32, HALF), low),
            pltpu.VMEM((NARROW, 16, HALF), low),
            pltpu.VMEM((2, 16, HALF), low),
            pltpu.VMEM((4, EXT, BLK), full),
            pltpu.VMEM((ELEMS, BLK), full),
            pltpu.VMEM((ELEMS, BLK), full),
            pltpu.SemaphoreType.DMA((GROUPS,)),
            pltpu.SemaphoreType.DMA((GROUPS,)),
            pltpu.SemaphoreType.DMA((3,)),
        ],
        compiler_params=pltpu.CompilerParams(
            collective_id=0, has_side_effects=True, vmem_limit_bytes=48 * 1024 * 1024
        ),
        name="migrate",
    )(coefficients, neighbours, halo_blocks.reshape(8), weights, info)
    return modal, metric, work.reshape(ELEMS)


def solution(mesh):
    return jax.shard_map(
        per_device,
        mesh=mesh,
        in_specs=(
            P(None, ("wide", "narrow")),
            P(None, ("wide", "narrow")),
            P(("wide", "narrow"), None, None),
            P(),
            P(("wide", "narrow")),
            P(("wide", "narrow")),
        ),
        out_specs=(P(None, ("wide", "narrow")), P(None, ("wide", "narrow")), P(("wide", "narrow"))),
        check_vma=False,
    )
```

time: 323 us -> 127 us (0.39)
  Pallas kernels: 0 us -> 119 us
  waiting for transfers between devices: 117 us -> 0 us
  local copies, waits for them, and re-layouts: 83.2 us -> 4.99 us
  starting transfers between devices: 71.7 us -> 0 us
  other arithmetic: 25.1 us -> 0.76 us
  blocking collectives: 16 us -> 0 us
  matrix products: 6.45 us -> 0 us
    pallas_call x0 -> x1, Pallas kernels: none -> 119 us  [per_device(): pl.pallas_call(kernel, out_shape=(jax.ShapeDtypeStruct((COEF, ELEMS), low...]
    all_to_all x4 -> x0, waiting for transfers between devices: 99.8 us -> none  [the longest x1 76.9 us: per_device(): lax.all_to_all(joined_coeffs, 'wide', split_axis=1, concat_axis=1, tiled=...]
    gather x21 -> x0, local copies, waits for them, and re-layouts: 70.6 us -> none  [the longest x4 56.8 us: per_device(): gathered = jnp.take(extended, neighbours[face_index], axis=1)]
    all_to_all x4 -> x0, starting transfers between devices: 46.5 us -> none  [the longest x1 20 us: per_device(): lax.all_to_all(pair_tags.astype(jnp.float32)[None, :], 'wide', split_axis...]
    ppermute x9 -> x0, starting transfers between devices: 25.1 us -> none  [the longest x4 12.7 us: passed_along(): return lax.ppermute(value, axis, pairs)]
    ppermute x9 -> x0, waiting for transfers between devices: 17.6 us -> none  [the longest x5 17.6 us: swapped(): lax.ppermute(value, axis, [(i, i ^ 1 << apart) for i in range(lax.axis_si...]
    all_to_all x1 -> x0, blocking collectives: 16 us -> none  [per_device(): lax.all_to_all(relayed_stats, 'narrow', split_axis=1, concat_axis=1, tile...]
    sort x3 -> x0, other arithmetic: 6.68 us -> none  [the longest x1 2.54 us: per_device(): jnp.argsort(jnp.where(anchor == other, 0, 1) * pair_total + pair_ids)]
  transfers between devices with their start and end apart: 13 -> 0, of which waited for: 5 -> 0; matrix products, arithmetic and copies ran while one was open for 11% -> 0% of each run, Pallas kernels for 0% -> 0%
where the time goes in v1:
time: 127 us; the launch traced here: 126 us
  Pallas kernels  119 us (94%)
  local copies, waits for them, and re-layouts  4.99 us (4%)
    pallas_call x1, Pallas kernels, per_device(): pl.pallas_call(kernel, out_shape=(jax.ShapeDtypeStruct((COEF, ELEMS), low...  119 us
    unnamed x9, local copies, waits for them, and re-layouts  3.62 us

profile of v1, /device:TPU:24, one launch (start us, length us, event | category | flops | bytes accessed | tf_op | source)
XLA Modules:
  0.0 125.9 jit_solution(14484879456540915571)
XLA Ops:
  0.6 0.0 copy-start
  0.7 0.8 multiply_add_fusion
  1.4 0.1 reshape_tile.3
  1.5 0.8 copy.11
  2.3 0.1 reshape.93.halo
  2.4 1.0 reshape.94
  3.4 0.0 copy-start.1
  3.4 0.2 copy.13.wts
  3.6 0.0 copy-done
  3.6 0.7 copy-done.1
  4.3 119.4 %migrate.1 = (bf16[100,4096]{1,0:T(8,128)(2,1)S(1)}, f32[6,4096]{1,0:T(8,128)S(1)}, f32[1,4096]{1,0:T(1,128)S(1)}) custom-call(bf16[100,4096]{1,0:T(8,128)(2,1)S(1)} %copy-done, s32[4,4096]{1,0:T(4,128)S(1)} %copy-done.1, s32[8]{0:T(128)S(1)} %reshape.93.halo, bf16[100,640]{1,0:T(8,128)(2,1)S(1)} %copy.13.wts, s32[1,128]{1,0:T(1,128)S(1)} %compare_select_fusion.info), custom_call_target="tpu_custom_call" | custom-call | tf_op jit(solution)/shard_map/migrate/pallas_call | solution.py:359
  123.7 0.9 copy.18
  124.6 0.7 copy.19
  125.3 0.6 copy.20
  (4 shorter events, 0.1 us)
Async XLA Ops:
  0.6 3.0 %copy-start = (bf16[100,4096]{1,0:T(8,128)(2,1)S(1)}, bf16[100,4096]{1,0:T(8,128)(2,1)}, u32[]{:S(2)}) copy-start(bf16[100,4096]{1,0:T(8,128)(2,1)} %coef.1) | copy-start | bytes 2457604
  3.4 0.8 copy-start.1

commit v2 on v1

--- a/solution.py
+++ b/solution.py
@@ -18,8 +18,9 @@
 CODE = 1024
 
 INFO, SWAP_A, SWAP_B, SWAP_C, HALO_UP, HALO_DOWN, HALO_LEFT, HALO_RIGHT = range(8)
-WIDE_TAG, WIDE_A, WIDE_B, SWAP_L, WIDE_L, NARROW_C, NARROW_A, NARROW_B, NARROW_L = range(8, 17)
-GROUPS = 17
+WIDE_TAG, WIDE_A, WIDE_B, WIDE_C, SWAP_L, SWAP_M, WIDE_L = range(8, 15)
+COUNTS, NARROW_A, NARROW_B, NARROW_C, NARROW_L = range(15, 20)
+GROUPS = 20
 
 
 def aligned(value, step):
@@ -27,10 +28,11 @@
 
 
 def kernel(
-    coef, nbr, halo, wts, info, modal, metric, work,
-    tiles, pair_a, pair_b, pair_c, late, pinfo, both, pick_v, pick_s, tab_v, tab_s, cnt_v, cnt_r, cnt_s,
-    hsend, hrecv, tags, tags2, send_a, recv_a, send_b, recv_b, send_l, recv_l,
-    out_a, out_b, out_l, last, table, own, rows, sent, came, local,
+    coef_in, nbr_in, halo, weights, owner, units, modal, last, cnt_r,
+    coef, nbr, wts, info,
+    tiles, pair_a, pair_b, pair_c, late, pinfo, both, pick_v, pick_s, tab_v, tab_s, cnt_v,
+    hsend, hrecv, tags, tags2, send_a, recv_a, send_b, recv_b, send_c, recv_c, send_l, recv_l,
+    out_a, out_b, out_c, out_l, table, own, rows, sent, came, local,
 ):
     w = lax.axis_index("wide")
     a = lax.axis_index("narrow")
@@ -49,6 +51,11 @@
     def wait_bytes(ref, sem):
         pltpu.make_async_copy(ref, ref, sem).wait()
 
+    fetch_coef = pltpu.make_async_copy(coef_in, coef, local.at[3])
+    fetch_coef.start()
+    fetch_nbr = pltpu.make_async_copy(nbr_in, nbr, local.at[4])
+    fetch_nbr.start()
+
     barrier = pltpu.get_barrier_semaphore()
 
     def greet(i, carry):
@@ -58,10 +65,13 @@
     for d in range(1, NARROW):
         pl.semaphore_signal(barrier, inc=1, device_id=(w, lax.rem(a + d, NARROW)), device_id_type=MESH)
     lax.fori_loop(1, WIDE, greet, 0)
-    pl.semaphore_wait(barrier, WIDE - 1 + NARROW - 1)
-
-    swap_info = remote(info, pinfo, INFO, w, partner)
-    swap_info.start()
+
+    lane1 = lax.broadcasted_iota(jnp.int32, (1, BLK), 1)
+    code = jnp.zeros((1, BLK), jnp.int32)
+    for b in range(BLOCKS):
+        code = jnp.where(lane1 == h * BLOCKS + b, owner[b] + CODE * units[b], code)
+    info[...] = code
+    fetch_coef.wait()
 
     def retile(b, carry):
         at = pl.ds(aligned(b * BLK, BLK), BLK)
@@ -72,11 +82,22 @@
         return carry
 
     lax.fori_loop(0, BLOCKS, retile, 0)
-    swaps = []
-    for k in range(3):
-        swap = remote(tiles.at[3 * (1 - h) + k], pairs[k].at[mine], SWAP_A + k, w, partner)
-        swap.start()
-        swaps.append(swap)
+    pl.semaphore_wait(barrier, WIDE - 1 + NARROW - 1)
+
+    swap_info = remote(info, pinfo, INFO, w, partner)
+    swap_info.start()
+    swaps = [
+        remote(tiles.at[3 * (1 - h) + k], pairs[k].at[mine], SWAP_A + k, w, partner)
+        for k in range(3)
+    ]
+    swaps[0].start()
+
+    def keep(b, carry):
+        for k in range(3):
+            pairs[k][h * BLOCKS + b] = tiles[3 * h + k, b]
+        return carry
+
+    lax.fori_loop(0, BLOCKS, keep, 0)
 
     places = [
         (lax.rem(w + WIDE - 1, WIDE), a),
@@ -87,19 +108,10 @@
     halos = []
     for k in range(4):
         for s in range(2):
-            block = halo[k * 2 + s]
+            block = halo[0, s, k]
             for r in range(7):
                 hsend[k, s, r] = tiles[r, block]
-        push = remote(hsend.at[k], hrecv.at[k ^ 1], HALO_UP + k, *places[k])
-        push.start()
-        halos.append(push)
-
-    def keep(b, carry):
-        for k in range(3):
-            pairs[k][h * BLOCKS + b] = tiles[3 * h + k, b]
-        return carry
-
-    lax.fori_loop(0, BLOCKS, keep, 0)
+        halos.append(remote(hsend.at[k], hrecv.at[k ^ 1], HALO_UP + k, *places[k]))
 
     swap_info.wait()
     both[...] = info[...] + pinfo[...]
@@ -121,28 +133,23 @@
 
         lax.fori_loop(1, WIDE, one, 0)
 
+    def send_chunk(pair, src, dst, group):
+        def pack(t, carry):
+            src[t] = pair[pick_s[0, t]]
+            return carry
+
+        lax.fori_loop(0, WIDE, pack, 0)
+        dst[w] = src[w]
+        spread(src, dst, group)
+
     swaps[0].wait()
-
-    def pack_a(t, carry):
-        send_a[t] = pair_a[pick_s[0, t]]
-        return carry
-
-    lax.fori_loop(0, WIDE, pack_a, 0)
-    recv_a[w] = send_a[w]
-    spread(send_a, recv_a, WIDE_A)
-
+    swaps[1].start()
+    swaps[2].start()
+    for push in halos:
+        push.start()
+    send_chunk(pair_a, send_a, recv_a, WIDE_A)
     swaps[1].wait()
-    swaps[2].wait()
-
-    def pack_b(t, carry):
-        send_b[t, 0:16] = pair_b[pick_s[0, t]]
-        send_b[t, 16:32] = pair_c[pick_s[0, t]]
-        return carry
-
-    lax.fori_loop(0, WIDE, pack_b, 0)
-    recv_b[w] = send_b[w]
-    spread(send_b, recv_b, WIDE_B)
-
+    send_chunk(pair_b, send_b, recv_b, WIDE_B)
     def one_tag(i, carry):
         remote(both, tags.at[w], WIDE_TAG, lax.rem(w + i, WIDE), a).start()
         return carry
@@ -162,6 +169,13 @@
         for f in range(4):
             table[f, at, :] = result[:, (f + 1) * BLK : (f + 2) * BLK]
         return carry
+
+    place_row = lax.broadcasted_iota(jnp.int32, (75, BLK), 0)
+    place_lane = lax.broadcasted_iota(jnp.int32, (75, BLK), 1)
+    order = (place_lane % 32 < 25) & (place_row == 3 * (place_lane % 32) + place_lane // 32)
+    order = order.astype(jnp.float32).astype(jnp.bfloat16)
+    for f in range(5):
+        wts[:, f * BLK : (f + 1) * BLK] = product(weights[f], order).astype(jnp.bfloat16)
 
     lax.fori_loop(0, BLOCKS, own_block, 0)
     for push in halos:
@@ -173,16 +187,22 @@
             for f in range(4):
                 table[f, first : first + BLK, :] = result[:, f * BLK : (f + 1) * BLK]
 
+    fetch_nbr.wait()
+
     def gather(i, carry):
-        for u in range(8):
-            e = i * 8 + u
+        for u in range(32):
+            e = i * 32 + u
             total = table[0, nbr[0, e]]
             for f in range(1, 4):
                 total = total + table[f, nbr[f, e]]
             rows[e] = total
         return carry
 
-    lax.fori_loop(0, ELEMS // 8, gather, 0)
+    lax.fori_loop(0, 64, gather, 0)
+    swaps[2].wait()
+    send_chunk(pair_c, send_c, recv_c, WIDE_C)
+
+    lax.fori_loop(64, 128, gather, 0)
 
     def metric_block(b, carry):
         at = pl.ds(aligned(b * BLK, BLK), BLK)
@@ -202,11 +222,15 @@
         late[h * BLOCKS + b] = tile.astype(jnp.bfloat16)
         return carry
 
-    lax.fori_loop(0, BLOCKS, metric_block, 0)
-
-    swap_late = remote(late.at[mine], late.at[mine], SWAP_L, w, partner)
-    swap_late.start()
-    swap_late.wait()
+    late_swaps = []
+    for part in range(2):
+        count_half = BLOCKS // 2
+        lax.fori_loop(part * count_half, (part + 1) * count_half, metric_block, 0)
+        half = late.at[pl.ds(h * BLOCKS + part * count_half, count_half)]
+        late_swaps.append(remote(half, half, SWAP_L + part, w, partner))
+        late_swaps[-1].start()
+    for swap in late_swaps:
+        swap.wait()
     odd = lax.rem(w + h, 2)
 
     def pack_l(i, carry):
@@ -264,7 +288,7 @@
     to_scalar.wait()
     cnt_r[a] = cnt_v[...]
     for d in range(1, NARROW):
-        remote(cnt_v, cnt_r.at[a], NARROW_C, w, lax.rem(a + d, NARROW)).start()
+        remote(cnt_v, cnt_r.at[a], COUNTS, w, lax.rem(a + d, NARROW)).start()
 
     def collect(src, dst):
         def one(s, carry):
@@ -277,17 +301,18 @@
 
     side = pl.ds(aligned(j * HALF, HALF), HALF)
 
-    def deliver(src, recv, out, first, tall, group):
+    def deliver(src, recv, out, first, group):
         wait_bytes(recv.at[pl.ds(0, WIDE - 1)], came.at[src])
         collect(recv, out)
-        place = pl.ds(aligned(first, 16), tall)
+        place = pl.ds(aligned(first, 16), 16)
         for d in range(1, NARROW):
             c = lax.rem(a + d, NARROW)
             remote(out.at[c], modal.at[place, side], group, w, c).start()
         modal[place, side] = out[a]
 
-    deliver(WIDE_A, recv_a, out_a, 48 * h, 16, NARROW_A)
-    deliver(WIDE_B, recv_b, out_b, 48 * h + 16, 32, NARROW_B)
+    deliver(WIDE_A, recv_a, out_a, 48 * h, NARROW_A)
+    deliver(WIDE_B, recv_b, out_b, 48 * h + 16, NARROW_B)
+    deliver(WIDE_C, recv_c, out_c, 48 * h + 32, NARROW_C)
 
     @pl.when(odd == 0)
     def _():
@@ -298,9 +323,7 @@
             remote(out_l.at[c], last.at[j], NARROW_L, w, c).start()
         last[j] = out_l[a]
 
-    wait_bytes(cnt_r.at[pl.ds(0, 3)], came.at[NARROW_C])
-    to_scalar = pltpu.make_async_copy(cnt_r, cnt_s, local.at[2])
-    to_scalar.start()
+    wait_bytes(cnt_r.at[pl.ds(0, 3)], came.at[COUNTS])
 
     @pl.when(odd == 0)
     def _():
@@ -309,30 +332,16 @@
     @pl.when(odd == 1)
     def _():
         wait_bytes(last, came.at[NARROW_L])
-
-    to_scalar.wait()
-    for p in range(2):
-        tiles = last[p].astype(jnp.float32)
-        full = tiles[0:8] + tiles[8:16]
-        metric[:, p * HALF : (p + 1) * HALF] = full[0:6]
-        modal[96:100, p * HALF : (p + 1) * HALF] = jnp.concatenate(
-            [tiles[6:8], tiles[14:16]], axis=0
-        ).astype(jnp.bfloat16)
-        xx, yy, zz = full[0:1], full[1:2], full[2:3]
-        xy, xz, yz = full[3:4], full[4:5], full[5:6]
-        det = xx * (yy * zz - yz * yz) - xy * (xy * zz - yz * xz) + xz * (xy * yz - yy * xz)
-        root = jnp.sqrt(det)
-        for s in range(16):
-            units = cnt_s[2 * p, (s // 8) * NARROW + a, s % 8].astype(jnp.float32)
-            first = p * HALF + s * BLK
-            work[:, first : first + BLK] = root[:, s * BLK : (s + 1) * BLK] * units
 
     wait_bytes(out_a.at[pl.ds(0, 3)], came.at[NARROW_A])
     wait_bytes(out_b.at[pl.ds(0, 3)], came.at[NARROW_B])
     wait_bytes(send_a.at[pl.ds(0, WIDE - 1)], sent.at[WIDE_A])
     wait_bytes(send_b.at[pl.ds(0, WIDE - 1)], sent.at[WIDE_B])
     wait_bytes(tags.at[pl.ds(0, WIDE - 1)], sent.at[WIDE_TAG])
-    wait_bytes(cnt_r.at[pl.ds(0, 3)], sent.at[NARROW_C])
+    wait_bytes(cnt_r.at[pl.ds(0, 3)], sent.at[COUNTS])
+    wait_bytes(send_c.at[pl.ds(0, WIDE - 1)], sent.at[WIDE_C])
+    wait_bytes(out_c.at[pl.ds(0, 3)], came.at[NARROW_C])
+    wait_bytes(out_c.at[pl.ds(0, 3)], sent.at[NARROW_C])
     wait_bytes(out_a.at[pl.ds(0, 3)], sent.at[NARROW_A])
     wait_bytes(out_b.at[pl.ds(0, 3)], sent.at[NARROW_B])
 
@@ -346,26 +355,42 @@
         wait_bytes(send_l.at[pl.ds(0, WIDE // 2)], sent.at[WIDE_L])
 
 
+def finish(moved, last, counts, modal, metric, work):
+    p = pl.program_id(0)
+    a = lax.axis_index("narrow")
+    modal[0:96] = moved[...]
+    tiles = last[0].astype(jnp.float32)
+    full = tiles[0:8] + tiles[8:16]
+    metric[...] = full[0:6]
+    modal[96:100] = jnp.concatenate([tiles[6:8], tiles[14:16]], axis=0).astype(jnp.bfloat16)
+    xx, yy, zz = full[0:1], full[1:2], full[2:3]
+    xy, xz, yz = full[3:4], full[4:5], full[5:6]
+    det = xx * (yy * zz - yz * yz) - xy * (xy * zz - yz * xz) + xz * (xy * yz - yy * xz)
+    root = jnp.sqrt(det)
+    for s in range(16):
+        units = counts[2 * p, (s // 8) * NARROW + a, s % 8].astype(jnp.float32)
+        work[:, s * BLK : (s + 1) * BLK] = root[:, s * BLK : (s + 1) * BLK] * units
+
+
 def per_device(coefficients, neighbours, halo_blocks, recon_weight, owner_device, work_count):
-    member = lax.axis_index("narrow") % 2
-    code = jnp.tile(owner_device + CODE * work_count, 4).reshape(1, BLK)
-    lane = lax.broadcasted_iota(jnp.int32, (1, BLK), 1)
-    info = jnp.where(lane // BLOCKS == member, code, 0)
-    weights = recon_weight.reshape(5, 25, 3, COEF).transpose(3, 0, 2, 1)
-    weights = jnp.pad(weights, ((0, 0), (0, 0), (0, 1), (0, 7))).reshape(COEF, 5 * BLK)
     vmem = pl.BlockSpec(memory_space=pltpu.VMEM)
     smem = pl.BlockSpec(memory_space=pltpu.SMEM)
+    hbm = pl.BlockSpec(memory_space=pl.ANY)
     low, full, whole = jnp.bfloat16, jnp.float32, jnp.int32
-    modal, metric, work = pl.pallas_call(
+    moved, last, counts = pl.pallas_call(
         kernel,
         out_shape=(
-            jax.ShapeDtypeStruct((COEF, ELEMS), low),
-            jax.ShapeDtypeStruct((6, ELEMS), full),
-            jax.ShapeDtypeStruct((1, ELEMS), full),
+            jax.ShapeDtypeStruct((96, ELEMS), low),
+            jax.ShapeDtypeStruct((2, 16, HALF), low),
+            jax.ShapeDtypeStruct((NARROW, 8, BLK), whole),
         ),
-        in_specs=[vmem, smem, smem, vmem, vmem],
+        in_specs=[hbm, hbm, smem, vmem, smem, smem],
         out_specs=(vmem, vmem, vmem),
         scratch_shapes=[
+            pltpu.VMEM((COEF, ELEMS), low),
+            pltpu.SMEM((4, ELEMS), whole),
+            pltpu.VMEM((COEF, 5 * BLK), low),
+            pltpu.VMEM((1, BLK), whole),
             pltpu.VMEM((7, BLOCKS, 16, BLK), low),
             pltpu.VMEM((2 * BLOCKS, 16, BLK), low),
             pltpu.VMEM((2 * BLOCKS, 16, BLK), low),
@@ -378,34 +403,54 @@
             pltpu.VMEM((8, BLK), whole),
             pltpu.SMEM((8, BLK), whole),
             pltpu.VMEM((8, BLK), whole),
-            pltpu.VMEM((NARROW, 8, BLK), whole),
-            pltpu.SMEM((NARROW, 8, BLK), whole),
             pltpu.VMEM((4, 2, 7, 16, BLK), low),
             pltpu.VMEM((4, 2, 7, 16, BLK), low),
             pltpu.VMEM((WIDE, 1, BLK), whole),
             pltpu.VMEM((WIDE, BLK), whole),
             pltpu.VMEM((WIDE, 16, BLK), low),
             pltpu.VMEM((WIDE, 16, BLK), low),
-            pltpu.VMEM((WIDE, 32, BLK), low),
-            pltpu.VMEM((WIDE, 32, BLK), low),
+            pltpu.VMEM((WIDE, 16, BLK), low),
+            pltpu.VMEM((WIDE, 16, BLK), low),
+            pltpu.VMEM((WIDE, 16, BLK), low),
+            pltpu.VMEM((WIDE, 16, BLK), low),
             pltpu.VMEM((WIDE, 16, BLK), low),
             pltpu.VMEM((WIDE, 16, BLK), low),
             pltpu.VMEM((NARROW, 16, HALF), low),
-            pltpu.VMEM((NARROW, 32, HALF), low),
             pltpu.VMEM((NARROW, 16, HALF), low),
-            pltpu.VMEM((2, 16, HALF), low),
+            pltpu.VMEM((NARROW, 16, HALF), low),
+            pltpu.VMEM((NARROW, 16, HALF), low),
             pltpu.VMEM((4, EXT, BLK), full),
             pltpu.VMEM((ELEMS, BLK), full),
             pltpu.VMEM((ELEMS, BLK), full),
             pltpu.SemaphoreType.DMA((GROUPS,)),
             pltpu.SemaphoreType.DMA((GROUPS,)),
-            pltpu.SemaphoreType.DMA((3,)),
+            pltpu.SemaphoreType.DMA((5,)),
         ],
         compiler_params=pltpu.CompilerParams(
-            collective_id=0, has_side_effects=True, vmem_limit_bytes=48 * 1024 * 1024
+            collective_id=0, has_side_effects=True, vmem_limit_bytes=63 * 1024 * 1024
         ),
         name="migrate",
-    )(coefficients, neighbours, halo_blocks.reshape(8), weights, info)
+    )(coefficients, neighbours, halo_blocks.transpose(0, 2, 1), recon_weight, owner_device, work_count)
+    modal, metric, work = pl.pallas_call(
+        finish,
+        grid=(2,),
+        out_shape=(
+            jax.ShapeDtypeStruct((COEF, ELEMS), low),
+            jax.ShapeDtypeStruct((6, ELEMS), full),
+            jax.ShapeDtypeStruct((1, ELEMS), full),
+        ),
+        in_specs=[
+            pl.BlockSpec((96, HALF), lambda p: (0, p)),
+            pl.BlockSpec((1, 16, HALF), lambda p: (p, 0, 0)),
+            smem,
+        ],
+        out_specs=(
+            pl.BlockSpec((COEF, HALF), lambda p: (0, p)),
+            pl.BlockSpec((6, HALF), lambda p: (0, p)),
+            pl.BlockSpec((1, HALF), lambda p: (0, p)),
+        ),
+        name="finish",
+    )(moved, last, counts)
     return modal, metric, work.reshape(ELEMS)
 
 

time: 127 us -> 119 us (0.937)
  local copies, waits for them, and re-layouts: 4.99 us -> 0 us
    unnamed x9 -> x0, local copies, waits for them, and re-layouts: 3.62 us -> none
    pallas_call x1 -> x2, Pallas kernels: 119 us -> 118 us  [the longest x1 116 us: per_device(): pl.pallas_call(kernel, out_shape=(jax.ShapeDtypeStruct((96, ELEMS), low),...]
where the time goes in v2:
time: 119 us
  Pallas kernels  118 us (99%)
    pallas_call x1, Pallas kernels, per_device(): pl.pallas_call(kernel, out_shape=(jax.ShapeDtypeStruct((96, ELEMS), low),...  116 us

profile of v2, /device:TPU:24, one launch (start us, length us, event | category | flops | bytes accessed | tf_op | source)
XLA Modules:
  0.0 119.1 jit_solution(15314512825006158057)
XLA Ops:
  0.6 116.3 %migrate.1 = (bf16[96,4096]{1,0:T(8,128)(2,1)}, bf16[2,16,2048]{2,1,0:T(8,128)(2,1)}, s32[4,8,128]{2,1,0:T(8,128)}) custom-call(bf16[100,4096]{1,0:T(8,128)(2,1)} %coef_in.1, s32[4,4096]{1,0:T(4,128)} %nbr_in.1, s32[1,2,4]{2,1,0:T(2,128)} %bitcast.2, bf16[5,75,100]{2,1,0:T(8,128)(2,1)} %weights.1, s32[32]{0:T(128)} %owner.1, s32[32]{0:T(128)} %units.1), custom_call_target="tpu_custom_call" | custom-call | tf_op jit(solution)/shard_map/migrate/pallas_call | solution.py:380
  117.0 2.1 %finish.1 = (bf16[100,4096]{1,0:T(8,128)(2,1)}, f32[6,4096]{1,0:T(8,128)}, f32[1,4096]{1,0:T(1,128)}) custom-call(bf16[96,4096]{1,0:T(8,128)(2,1)} %get-tuple-element.9.moved, bf16[2,16,2048]{2,1,0:T(8,128)(2,1)} %get-tuple-element.10.last, s32[4,8,128]{2,1,0:T(8,128)} %get-tuple-element.11.counts), custom_call_target="tpu_custom_call" | custom-call | tf_op jit(solution)/shard_map/finish/pallas_call | solution.py:434

commit v3 on v2

--- a/solution.py
+++ b/solution.py
@@ -25,6 +25,24 @@
 
 def aligned(value, step):
     return pl.multiple_of(value, step)
+
+
+def eights(step):
+    def some(i, carry):
+        for u in range(8):
+            carry = step(8 * i + u, carry)
+        return carry
+
+    return some
+
+
+def sevens(step):
+    def some(i, carry):
+        for u in range(7):
+            carry = step(7 * i + u + 1, carry)
+        return carry
+
+    return some
 
 
 def kernel(
@@ -64,7 +82,8 @@
 
     for d in range(1, NARROW):
         pl.semaphore_signal(barrier, inc=1, device_id=(w, lax.rem(a + d, NARROW)), device_id_type=MESH)
-    lax.fori_loop(1, WIDE, greet, 0)
+    lax.fori_loop(0, 18, sevens(greet), 0)
+    greet(WIDE - 1, 0)
 
     lane1 = lax.broadcasted_iota(jnp.int32, (1, BLK), 1)
     code = jnp.zeros((1, BLK), jnp.int32)
@@ -131,14 +150,15 @@
             remote(src.at[t], dst.at[w], group, t, a).start()
             return carry
 
-        lax.fori_loop(1, WIDE, one, 0)
+        lax.fori_loop(0, 18, sevens(one), 0)
+        one(WIDE - 1, 0)
 
     def send_chunk(pair, src, dst, group):
         def pack(t, carry):
             src[t] = pair[pick_s[0, t]]
             return carry
 
-        lax.fori_loop(0, WIDE, pack, 0)
+        lax.fori_loop(0, WIDE // 8, eights(pack), 0)
         dst[w] = src[w]
         spread(src, dst, group)
 
@@ -190,12 +210,16 @@
     fetch_nbr.wait()
 
     def gather(i, carry):
-        for u in range(32):
-            e = i * 32 + u
-            total = table[0, nbr[0, e]]
-            for f in range(1, 4):
-                total = total + table[f, nbr[f, e]]
-            rows[e] = total
+        for group in range(4):
+            totals = []
+            for u in range(8):
+                e = i * 32 + group * 8 + u
+                total = table[0, nbr[0, e]]
+                for f in range(1, 4):
+                    total = total + table[f, nbr[f, e]]
+                totals.append(total)
+            for u in range(8):
+                rows[i * 32 + group * 8 + u] = totals[u]
         return carry
 
     lax.fori_loop(0, 64, gather, 0)
@@ -238,7 +262,7 @@
         send_l[t] = late[pick_s[0, t]]
         return carry
 
-    lax.fori_loop(0, WIDE // 2, pack_l, 0)
+    lax.fori_loop(0, WIDE // 16, eights(pack_l), 0)
 
     def send_late(i, carry):
         t = lax.rem(w + 2 * i + odd, WIDE)
@@ -257,7 +281,7 @@
         tags2[pl.ds(i, 1), :] = tags[i]
         return carry
 
-    lax.fori_loop(0, WIDE, flat, 0)
+    lax.fori_loop(0, WIDE // 8, eights(flat), 0)
     codes = jnp.transpose(tags2[...])
     here = (codes >= CODE) & ((codes & (CODE - 1)) // NARROW == w)
     kinds = jnp.where(here, (sub // BLOCKS) * NARROW + lax.rem(codes, NARROW) + 1, 0)
@@ -297,7 +321,7 @@
                 dst[c, :, at] = src[tab_s[(s // 8) * NARROW + c, lax.rem(s, 8)]]
             return carry
 
-        lax.fori_loop(0, 16, one, 0)
+        lax.fori_loop(0, 2, eights(one), 0)
 
     side = pl.ds(aligned(j * HALF, HALF), HALF)
 

time: 119 us -> 118 us (level)
  no operation moved by 1% of the time
where the time goes in v3:
time: 118 us
  Pallas kernels  117 us (99%)
    pallas_call x1, Pallas kernels, per_device(): pl.pallas_call(kernel, out_shape=(jax.ShapeDtypeStruct((96, ELEMS), low),...  115 us

profile of v3, /device:TPU:24, one launch (start us, length us, event | category | flops | bytes accessed | tf_op | source)
XLA Modules:
  0.0 118.0 jit_solution(9201698133834218671)
XLA Ops:
  0.6 115.3 %migrate.1 = (bf16[96,4096]{1,0:T(8,128)(2,1)}, bf16[2,16,2048]{2,1,0:T(8,128)(2,1)}, s32[4,8,128]{2,1,0:T(8,128)}) custom-call(bf16[100,4096]{1,0:T(8,128)(2,1)} %coef_in.1, s32[4,4096]{1,0:T(4,128)} %nbr_in.1, s32[1,2,4]{2,1,0:T(2,128)} %bitcast.2, bf16[5,75,100]{2,1,0:T(8,128)(2,1)} %weights.1, s32[32]{0:T(128)} %owner.1, s32[32]{0:T(128)} %units.1), custom_call_target="tpu_custom_call" | custom-call | tf_op jit(solution)/shard_map/migrate/pallas_call | solution.py:404
  115.9 2.1 %finish.1 = (bf16[100,4096]{1,0:T(8,128)(2,1)}, f32[6,4096]{1,0:T(8,128)}, f32[1,4096]{1,0:T(1,128)}) custom-call(bf16[96,4096]{1,0:T(8,128)(2,1)} %get-tuple-element.9.moved, bf16[2,16,2048]{2,1,0:T(8,128)(2,1)} %get-tuple-element.10.last, s32[4,8,128]{2,1,0:T(8,128)} %get-tuple-element.11.counts), custom_call_target="tpu_custom_call" | custom-call | tf_op jit(solution)/shard_map/finish/pallas_call | solution.py:458
